TPU v7x, 32 devices: a whole 2x2x4 slice. The times are simulated.
32 devices in a mesh: groups: 2 (over y), dp: 4 (over z), query: 2 (over x), mp: 2 (over core).
Axes of the slice: x: 2, y: 2, z: 4, core: 2. Of those that a mesh axis runs over, the one named last changes fastest.
Arguments:
- hidden_in: bfloat16 [16, 192, 14336], P(('groups', 'dp'), 'query', 'mp'), parts along dimension 0, may hold values from -6 to 6
- out_grad: bfloat16 [16, 192, 4096], P(('groups', 'dp'), 'query', 'mp'), parts along dimension 0, may hold values from -6 to 6
- proj_in: bfloat16 [32, 14336], P(None, 'mp'), may hold values from -0.046875 to 0.046875
- proj_out: bfloat16 [32, 4096], P(None, 'mp'), may hold values from -0.09375 to 0.09375
- lengths: int32 [16], P(('groups', 'dp')), parts along dimension 0, may hold values from 48 to 192
- query_grads: float32 [512, 1024], P(('groups', 'query', 'dp')), parts along dimension 0, may hold values from -4 to 4
Outputs:
- scores: float32 [16, 256], P(('groups', 'dp'), 'query'), parts along dimension 0
There are 2 independent parts, one for each index of `groups`. A program takes and returns all parts, laid end to end along the dimension named above; an argument that names none is the same for every part. Nothing has to cross between parts.
All inputs are finite; a program needn't handle non-finite values.
Results may differ from a plain program's by a relative error of at most 0.00035.
Values sent between devices are 32-bit elements; how exact they have to be, the bound alone decides.
A program may use at most 64 MiB of HBM per device.

v0:
```python
import jax
import jax.numpy as jnp
from jax import lax
from jax.sharding import PartitionSpec as P

DAMPING = 1.0


def chol_apply(factor, rhs):
    middle = lax.linalg.triangular_solve(factor, rhs, left_side=True, lower=True)
    return lax.linalg.triangular_solve(factor, middle, left_side=True, lower=True, transpose_a=True)


def shards(hidden_in, out_grad, proj_in, proj_out, lengths, query_grads):
    ex_count, seq_count, _ = hidden_in.shape
    proj_rank = proj_in.shape[0]
    flat_size = proj_rank * proj_rank
    row_count = ex_count * seq_count
    contract = (((1,), (1,)), ((), ()))
    in_proj = lax.dot_general(
        hidden_in.reshape(row_count, -1), proj_in, contract, preferred_element_type=jnp.float32
    )
    out_proj = lax.dot_general(
        out_grad.reshape(row_count, -1), proj_out, contract, preferred_element_type=jnp.float32
    )
    out_local, in_local = (
        lax.psum_scatter(out_proj, "mp", scatter_dimension=0, tiled=True),
        lax.psum_scatter(in_proj, "mp", scatter_dimension=0, tiled=True),
    )
    half_rows = row_count // lax.axis_size("mp")
    row_ids = lax.axis_index("mp") * half_rows + jnp.arange(half_rows)
    example_ids = row_ids // seq_count
    positions = lax.axis_index("query") * seq_count + row_ids % seq_count
    membership = (example_ids[None, :] == jnp.arange(ex_count)[:, None]) & (
        positions[None, :] < lengths[:, None]
    )
    weights = (
        jnp.where(membership, 1.0, 0.0).astype(jnp.float32)
        / jnp.sqrt(lengths.astype(jnp.float32))[:, None]
    )
    weighted = weights[:, :, None] * out_local[None, :, :]
    partial_grads = jnp.einsum(
        "eri,rj->eij", weighted, in_local, precision=lax.Precision.HIGHEST
    ).reshape(ex_count, flat_size)
    shares = lax.psum_scatter(partial_grads, ("query", "mp"), scatter_dimension=1, tiled=True)
    vectors = lax.all_gather(shares, ("query", "mp"), axis=1, tiled=True)
    total_examples = ex_count * lax.axis_size("dp")
    all_vectors = lax.all_gather(vectors, "dp", axis=0, tiled=True)
    gram_matrix = jnp.dot(all_vectors, all_vectors.T, precision=lax.Precision.HIGHEST)
    gram_matrix = gram_matrix + DAMPING * total_examples * jnp.eye(
        total_examples, dtype=jnp.float32
    )
    factor = jnp.linalg.cholesky(gram_matrix)
    coeffs = chol_apply(
        factor, jnp.dot(all_vectors, query_grads.T, precision=lax.Precision.HIGHEST)
    )
    prepared = (
        query_grads - jnp.dot(coeffs.T, all_vectors, precision=lax.Precision.HIGHEST)
    ) / DAMPING
    return jnp.dot(
        vectors,
        lax.all_gather(prepared, "dp", axis=0, tiled=True).T,
        precision=lax.Precision.HIGHEST,
    )


def solution(mesh):
    in_specs = (
        P(("groups", "dp"), "query", "mp"),
        P(("groups", "dp"), "query", "mp"),
        P(None, "mp"),
        P(None, "mp"),
        P(("groups", "dp")),
        P(("groups", "query", "dp"), None),
    )
    out_specs = P(("groups", "dp"), "query")
    return jax.shard_map(shards, mesh=mesh, in_specs=in_specs, out_specs=out_specs, check_vma=False)
```

profile of v0, /device:TPU:0, one launch (start us, length us, event | category | flops | bytes accessed | tf_op | source)
XLA Modules:
  0.0 102.7 jit_solution(15271839218335112503)
XLA Ops:
  6.5 0.0 copy-start
  6.5 0.0 reduce-scatter.10.cloned.1.call-start
  6.5 2.3 %fusion.15 = f32[192,32]{1,0:T(8,128)} fusion(bf16[192,2048]{1,0:T(8,128)(2,1)} %bitcast.44, bf16[32,2048]{1,0:T(8,128)(2,1)} %param.9), kind=kOutput, calls=%fused_computation.28 | convolution fusion | flops 25165824 | bytes 942080
  8.8 0.0 reduce-scatter.10.cloned.1.call-update
  8.8 0.0 reduce-scatter.12.cloned.1.call-start
  8.9 2.5 %fusion.16 = f32[192,32]{1,0:T(8,128)} fusion(bf16[192,7168]{1,0:T(8,128)(2,1)S(1)} %bitcast.42, bf16[32,7168]{1,0:T(8,128)(2,1)} %param.8), kind=kOutput, calls=%fused_computation.29 | convolution fusion | flops 88080384 | bytes 3235840
  11.4 0.0 reduce-scatter.12.cloned.1.call-update
  11.4 0.0 reduce-scatter.14.cloned.1.call-start
  11.5 0.1 fusion.12
  11.6 8.2 %reduce-scatter.10.cloned.1.call-done = f32[96,32]{1,0:T(8,128)} async-done(((f32[192,32]{1,0:T(8,128)}), f32[96,32]{1,0:T(8,128)}) %reduce-scatter.10.cloned.1.call-update) | async-done | bytes 12304
  19.8 0.9 copy.12
  20.6 10.0 %reduce-scatter.12.cloned.1.call-done = f32[96,32]{1,0:T(8,128)} async-done(((f32[192,32]{1,0:T(8,128)}), f32[96,32]{1,0:T(8,128)}) %reduce-scatter.12.cloned.1.call-update) | async-done | bytes 12304
  30.6 1.0 fusion
  31.6 1.1 %copy.17 = f32[2,32,32]{0,2,1:T(8,128)} copy(f32[2,32,32]{2,1,0:T(8,128)S(1)} %fusion) | data formatting | bytes 16384
  32.7 0.0 reduce-scatter.14.cloned.1.call-update
  32.7 23.3 %reduce-scatter.14.cloned.1.call-done = f32[256,2]{1,0:T(8,128)} async-done(((f32[1024,2]{1,0:T(8,128)}), f32[256,2]{1,0:T(8,128)}) %reduce-scatter.14.cloned.1.call-update) | async-done | bytes 2064
  56.0 1.0 copy.16
  57.0 5.2 %all_gather.9 = f32[2,1024]{1,0:T(2,128)S(1)} all-gather(f32[2,256]{1,0:T(2,128)S(1)} %copy.16), channel_id=1, replica_groups=mesh['groups'=2,'dp'=4,'query'=2,'mp'=2] {'query','mp'}, dimensions={1}, use_global_device_ids=true | all-gather | bytes 10240 | tf_op jit(solution)/shard_map/all_gather | solution.py:46
  62.1 13.1 %all-gather = f32[4,2,1024]{2,1,0:T(2,128)S(1)} all-gather(f32[1,2,1024]{2,1,0:T(2,128)S(1)} %bitcast.46), channel_id=1, replica_groups=mesh['groups'=2,'dp'=4,'query'=2,'mp'=2] {'dp'}, dimensions={0}, use_global_device_ids=true | all-gather | bytes 40960 | tf_op jit(solution)/shard_map/all_gather | solution.py:48
  75.3 0.1 fusion.17
  75.4 0.1 copy.9
  75.5 0.7 cholesky.16
  76.2 0.1 select_reduce_fusion
  76.3 0.6 compare_reduce_fusion
  76.9 0.6 fusion.5
  77.6 0.6 custom-call.8
  78.2 0.2 fusion.18
  78.4 0.2 fusion.6
  78.6 0.1 fusion.8
  78.8 0.3 convolution_subtract_fusion
  79.1 16.0 %all_gather.11 = f32[128,1024]{1,0:T(8,128)S(1)} all-gather(f32[32,1024]{1,0:T(8,128)S(1)} %convolution_subtract_fusion), channel_id=1, replica_groups=mesh['groups'=2,'dp'=4,'query'=2,'mp'=2] {'dp'}, dimensions={0}, use_global_device_ids=true | all-gather | bytes 655360 | tf_op jit(solution)/shard_map/all_gather | solution.py:62
  95.1 1.1 %fusion.19 = f32[2,128]{1,0:T(2,128)} fusion(f32[2,1024]{1,0:T(2,128)S(1)} %all_gather.9, f32[128,1024]{1,0:T(8,128)S(1)} %all_gather.11), kind=kOutput, calls=%fused_computation.32 | convolution fusion | flops 3145728 | bytes 533504 | tf_op jit(solution)/shard_map/dot_general | solution.py:60
  (9 shorter events, 0.1 us)
Async XLA Ops:
  6.5 2.4 %copy-start = (bf16[2,96,7168]{2,1,0:T(8,128)(2,1)S(1)}, bf16[2,96,7168]{2,1,0:T(8,128)(2,1)}, u32[]{:S(2)}) copy-start(bf16[2,96,7168]{2,1,0:T(8,128)(2,1)} %param.6) | copy-start | bytes 8257540
  6.5 4.9 %copy-start.2 = (s32[2]{0:T(128)S(1)}, s32[2]{0:T(128)}, u32[]{:S(2)}) copy-start(s32[2]{0:T(128)} %param.10) | copy-start | bytes 28
  6.5 13.2 %reduce-scatter.10.cloned.1.call-start = ((), (), s32[]{:S(2)}) async-start(), calls=%async_computation.3 | async-start | bytes 147456
  8.8 69.4 %copy-start.1 = (f32[32,1024]{1,0:T(8,128)S(1)}, f32[32,1024]{1,0:T(8,128)}, u32[]{:S(2)}) copy-start(f32[32,1024]{1,0:T(8,128)} %param.11) | copy-start | bytes 393220
  8.8 21.8 %reduce-scatter.12.cloned.1.call-start = ((), (), s32[]{:S(2)}) async-start(), calls=%async_computation.4 | async-start | bytes 147456
  11.4 44.6 %reduce-scatter.14.cloned.1.call-start = ((), (), s32[]{:S(2)}) async-start(), calls=%async_computation.5 | async-start | bytes 655360
Sparse Core Ops, SparseCore 0:
  9.6 10.1 reduce-scatter.9
  22.0 8.6 reduce-scatter.11
  33.1 22.8 reduce-scatter.13
where the time goes:
time: 103 us
  waiting for transfers between devices  41.5 us (40%)
  blocking collectives  34.3 us (33%)
  between operations  13.2 us (13%)
  matrix products  7.84 us (8%)
  local copies, waits for them, and re-layouts  3 us (3%)
  other arithmetic  2.81 us (3%)
    unnamed x6, waiting for transfers between devices  41.5 us
    all_gather x1, blocking collectives, shards(): lax.all_gather(prepared, 'dp', axis=0, tiled=True)  16 us
    all_gather x1, blocking collectives, shards(): all_vectors = lax.all_gather(vectors, 'dp', axis=0, tiled=True)  13.1 us
    all_gather x1, blocking collectives, shards(): vectors = lax.all_gather(shares, ('query', 'mp'), axis=1, tiled=True)  5.16 us
    unnamed x2, matrix products  4.77 us
    unnamed x10, local copies, waits for them, and re-layouts  2.93 us
  transfers between devices with their start and end apart: 3, of which 3 were waited for; matrix products, arithmetic and copies ran while one was open for 3% of the time, Pallas kernels for 0%

commit v1 on v0

v1 whole, which is shorter than its diff:
```python
import functools

import jax
import jax.numpy as jnp
from jax import lax
from jax.experimental import pallas as pl
from jax.experimental.pallas import tpu as pltpu
from jax.sharding import PartitionSpec as P

DAMPING = 1.0
LANES = 128
SUBLANES = 8
MESH = pl.DeviceIdType.MESH
LAST = (((1,), (1,)), ((), ()))


def dot_last(left, right, precision=None):
    return lax.dot_general(
        left, right, LAST, precision=precision, preferred_element_type=jnp.float32
    )


def each(count, body):
    if count <= 16:
        for step in range(1, count):
            body(step)
    else:
        lax.fori_loop(1, count, lambda step, carry: (body(step), carry)[1], 0)


def solve_few(vectors, rhs, shift):
    total, width = rhs.shape
    rows = lax.broadcasted_iota(jnp.int32, (total, width), 0)
    columns = []
    for j in range(total):
        column = jnp.sum(vectors * vectors[j : j + 1], axis=1, keepdims=True)
        column = jnp.broadcast_to(column, (total, width))
        columns.append(jnp.where(rows == j, column + shift, column))
    for k in range(total):
        pivot = columns[k]
        inverse = 1.0 / pivot[k : k + 1]

        def step(array):
            own = array[k : k + 1] * inverse
            return jnp.where(rows == k, own, array - pivot * own)

        rhs = step(rhs)
        columns = [step(c) if j > k else c for j, c in enumerate(columns)]
    return rhs


def solve_many(vectors, rhs, shift):
    total, width = rhs.shape
    gram = dot_last(vectors, vectors, lax.Precision.HIGHEST)
    rows = lax.broadcasted_iota(jnp.int32, (total, total), 0)
    columns = lax.broadcasted_iota(jnp.int32, (total, total), 1)
    rhs_rows = lax.broadcasted_iota(jnp.int32, (total, width), 0)
    gram = jnp.where(rows == columns, gram + shift, gram)

    def step(k, carry):
        gram, rhs = carry
        column = jnp.sum(jnp.where(columns == k, gram, 0.0), axis=1, keepdims=True)
        row = jnp.sum(jnp.where(rows == k, gram, 0.0), axis=0, keepdims=True)
        rhs_row = jnp.sum(jnp.where(rhs_rows == k, rhs, 0.0), axis=0, keepdims=True)
        pivot = jnp.sum(
            jnp.where(columns[:1] == k, row, 0.0), axis=1, keepdims=True
        )
        row, rhs_row = row / pivot, rhs_row / pivot
        gram = jnp.where(rows == k, row, gram - column * row)
        rhs = jnp.where(rhs_rows == k, rhs_row, rhs - column * rhs_row)
        return gram, rhs

    return lax.fori_loop(0, total, step, (gram, rhs))[1]


def kernel(
    sizes,
    chunks,
    hidden_hbm,
    grad_hbm,
    proj_in_hbm,
    proj_out_hbm,
    lengths_ref,
    query_hbm,
    out_ref,
    hidden,
    grad,
    proj_in,
    proj_out,
    query,
    sums,
    pair,
    grads,
    sent,
    landed,
    load_sem,
    hidden_sem,
    pair_send,
    pair_recv,
    grads_send,
    grads_recv,
    score_send,
    score_recv,
):
    dp_size, query_size, mp_size = sizes
    assert mp_size == 2
    my_dp, my_query, my_mp = (lax.axis_index(a) for a in ("dp", "query", "mp"))
    other = 1 - my_mp
    examples, seq, width = hidden.shape
    rank = proj_in.shape[0]
    queries = query.shape[0]
    planes = dp_size * query_size
    me = my_query * dp_size + my_dp
    total = dp_size * examples
    repeat = LANES // rank
    pieces = rank // repeat
    step_width = width // chunks

    def load(source, target, sem):
        copy = pltpu.make_async_copy(source, target, sem)
        copy.start()
        return copy

    proj_out_copy = load(proj_out_hbm, proj_out, load_sem.at[0])
    grad_copy = load(grad_hbm, grad, load_sem.at[1])
    hidden_copies = []
    for c in range(chunks):
        part = pl.ds(c * step_width, step_width)
        hidden_copies.append(
            (
                load(proj_in_hbm.at[:, part], proj_in.at[:, part], hidden_sem.at[0, c]),
                load(hidden_hbm.at[:, :, part], hidden.at[:, :, part], hidden_sem.at[1, c]),
            )
        )
    query_copy = load(query_hbm, query, load_sem.at[2])

    barrier = pltpu.get_barrier_semaphore()

    def place(step):
        slot = lax.rem(me + step, planes)
        return slot, {"dp": lax.rem(slot, dp_size), "query": slot // dp_size}

    def greet(step):
        pl.semaphore_signal(barrier, inc=1, device_id=place(step)[1], device_id_type=MESH)

    pl.semaphore_signal(barrier, inc=1, device_id={"mp": other}, device_id_type=MESH)
    each(planes, greet)

    proj_out_copy.wait()
    to_row = lax.broadcasted_iota(jnp.int32, (rank, rank), 0)
    from_row = lax.broadcasted_iota(jnp.int32, (rank, rank), 1)
    wanted = repeat * lax.rem(to_row, pieces) + to_row // pieces
    order = jnp.where(from_row == wanted, 1.0, 0.0).astype(jnp.bfloat16)
    ordered = jnp.dot(
        order, proj_out[...], preferred_element_type=jnp.float32
    ).astype(jnp.bfloat16)
    grad_copy.wait()
    for e in range(examples):
        sums[0, e] = dot_last(ordered, grad[e])

    pl.semaphore_wait(barrier, planes)

    def exchange(which):
        copy = pltpu.make_async_remote_copy(
            src_ref=sums.at[which],
            dst_ref=pair.at[which],
            send_sem=pair_send.at[which],
            recv_sem=pair_recv.at[which],
            device_id={"mp": other},
            device_id_type=MESH,
        )
        copy.start()
        return copy

    out_exchange = exchange(0)
    in_sums = [jnp.zeros((rank, seq), jnp.float32) for _ in range(examples)]
    for c in range(chunks):
        for copy in hidden_copies[c]:
            copy.wait()
        part = pl.ds(c * step_width, step_width)
        for e in range(examples):
            in_sums[e] += dot_last(proj_in[:, part], hidden[e, :, part])
    for e in range(examples):
        sums[1, e] = in_sums[e]
    in_exchange = exchange(1)
    query_copy.wait()
    out_exchange.wait()
    positions = my_query * seq + lax.broadcasted_iota(jnp.int32, (1, seq), 1)
    weighted = []
    for e in range(examples):
        used = jnp.full((1, seq), lengths_ref[e], jnp.int32)
        weights = jnp.where(positions < used, 1.0 / jnp.sqrt(used.astype(jnp.float32)), 0.0)
        weighted.append((sums[0, e] + pair[0, e]) * weights)
    in_exchange.wait()
    lanes = lax.broadcasted_iota(jnp.int32, (pieces, LANES), 1) // rank
    for e in range(examples):
        inputs = sums[1, e] + pair[1, e]
        product = dot_last(
            weighted[e], jnp.concatenate([inputs] * repeat, axis=0), lax.Precision.HIGHEST
        )
        flat = product[:pieces]
        for r in range(1, repeat):
            flat = jnp.where(lanes == r, product[r * pieces : (r + 1) * pieces], flat)
        grads[me, e * pieces : (e + 1) * pieces] = flat

    def grads_copy(slot, target):
        return pltpu.make_async_remote_copy(
            src_ref=grads.at[slot],
            dst_ref=grads.at[slot],
            send_sem=grads_send.at[target],
            recv_sem=grads_recv.at[slot],
            device_id=target_id(target),
            device_id_type=MESH,
        )

    def target_id(slot):
        return {"dp": lax.rem(slot, dp_size), "query": slot // dp_size}

    def send_grads(step):
        grads_copy(me, place(step)[0]).start()

    def wait_grads(step):
        slot = place(step)[0]
        grads_copy(slot, slot).wait_recv()

    def wait_sent(step):
        grads_copy(me, place(step)[0]).wait_send()

    each(planes, send_grads)
    each(planes, wait_grads)

    pieces_of = []
    flat_grads = grads.reshape(planes * examples * pieces, LANES)
    for p in range(pieces):
        piece = flat_grads[pl.ds(p, total, stride=pieces)]
        for q in range(1, query_size):
            piece += flat_grads[pl.ds(q * total * pieces + p, total, stride=pieces)]
        pieces_of.append(piece)
    vectors = jnp.concatenate(pieces_of, axis=1)
    blocks = LANES // queries
    rhs = dot_last(
        vectors, jnp.concatenate([query[...]] * blocks, axis=0), lax.Precision.HIGHEST
    )
    shift = DAMPING * total
    solve = solve_few if total <= SUBLANES else solve_many
    solved = solve(vectors, rhs * shift, shift)
    block_of_lane = lax.broadcasted_iota(jnp.int32, (total, LANES), 1) // queries
    solved = jnp.where(block_of_lane == lax.rem(my_dp, blocks), solved, 0.0)
    for d in range(dp_size):
        sent[d, :examples] = solved[d * examples : (d + 1) * examples]

    def score_copy(slot, target):
        return pltpu.make_async_remote_copy(
            src_ref=sent.at[target],
            dst_ref=landed.at[slot],
            send_sem=score_send.at[target],
            recv_sem=score_recv.at[slot],
            device_id={"dp": target},
            device_id_type=MESH,
        )

    def send_score(step):
        score_copy(my_dp, lax.rem(my_dp + step, dp_size)).start()

    def wait_score(step):
        slot = lax.rem(my_dp + step, dp_size)
        score_copy(slot, slot).wait_recv()

    def wait_score_sent(step):
        score_copy(my_dp, lax.rem(my_dp + step, dp_size)).wait_send()

    each(dp_size, send_score)
    landed[my_dp] = sent[my_dp]
    each(planes, wait_sent)
    each(dp_size, wait_score)
    for b in range(dp_size // blocks):
        block = landed[b * blocks]
        for d in range(b * blocks + 1, (b + 1) * blocks):
            block += landed[d]
        out_ref[:, b * LANES : (b + 1) * LANES] = block[:examples]
    each(dp_size, wait_score_sent)


def shards(sizes, hidden_in, out_grad, proj_in, proj_out, lengths, query_grads):
    dp_size, query_size, _ = sizes
    examples, seq, _ = hidden_in.shape
    rank = proj_in.shape[0]
    queries, flat = query_grads.shape
    planes = dp_size * query_size
    pieces = flat // LANES
    chunks = 4
    hbm = pl.BlockSpec(memory_space=pl.ANY)
    dma = pltpu.SemaphoreType.DMA
    sums = pltpu.VMEM((2, examples, rank, seq), jnp.float32)
    scores = pltpu.VMEM((dp_size, SUBLANES, LANES), jnp.float32)
    return pl.pallas_call(
        functools.partial(kernel, sizes, chunks),
        out_shape=jax.ShapeDtypeStruct((examples, dp_size * queries), jnp.float32),
        in_specs=[hbm, hbm, hbm, hbm, pl.BlockSpec(memory_space=pltpu.SMEM), hbm],
        out_specs=pl.BlockSpec(memory_space=pltpu.VMEM),
        scratch_shapes=[
            pltpu.VMEM(hidden_in.shape, hidden_in.dtype),
            pltpu.VMEM(out_grad.shape, out_grad.dtype),
            pltpu.VMEM(proj_in.shape, proj_in.dtype),
            pltpu.VMEM(proj_out.shape, proj_out.dtype),
            pltpu.VMEM(query_grads.shape, query_grads.dtype),
            sums,
            sums,
            pltpu.VMEM((planes, examples * pieces, LANES), jnp.float32),
            scores,
            scores,
            dma((3,)),
            dma((2, chunks)),
            dma((2,)),
            dma((2,)),
            dma((planes,)),
            dma((planes,)),
            dma((dp_size,)),
            dma((dp_size,)),
        ],
        compiler_params=pltpu.CompilerParams(
            collective_id=0, has_side_effects=True, vmem_limit_bytes=32 * 1024 * 1024
        ),
    )(hidden_in, out_grad, proj_in, proj_out, lengths, query_grads)


def solution(mesh):
    sizes = tuple(mesh.shape[a] for a in ("dp", "query", "mp"))
    in_specs = (
        P(("groups", "dp"), "query", "mp"),
        P(("groups", "dp"), "query", "mp"),
        P(None, "mp"),
        P(None, "mp"),
        P(("groups", "dp")),
        P(("groups", "query", "dp"), None),
    )
    out_specs = P(("groups", "dp"), "query")
    return jax.shard_map(
        functools.partial(shards, sizes),
        mesh=mesh,
        in_specs=in_specs,
        out_specs=out_specs,
        check_vma=False,
    )
```

time: 103 us -> 25.9 us (0.25)
  waiting for transfers between devices: 41.5 us -> 0 us
  blocking collectives: 34.3 us -> 0 us
  Pallas kernels: 0 us -> 18.7 us
  between operations: 13.2 us -> 0.02 us
  matrix products: 7.84 us -> 0 us
  local copies, waits for them, and re-layouts: 3 us -> 6.95 us
  other arithmetic: 2.81 us -> 0 us
    unnamed x6 -> x0, waiting for transfers between devices: 41.5 us -> none
    all_gather x3 -> x0, blocking collectives: 34.3 us -> none  [the longest x1 16 us: shards(): lax.all_gather(prepared, 'dp', axis=0, tiled=True)]
    pallas_call x0 -> x1, Pallas kernels: none -> 18.7 us  [shards(): pl.pallas_call(functools.partial(kernel, sizes, chunks), out_shape=jax.Sh...]
    unnamed x2 -> x0, matrix products: 4.77 us -> none
    unnamed x10 -> x13, local copies, waits for them, and re-layouts: 2.93 us -> 6.95 us
    another operation x5 -> x0, other arithmetic: 2.7 us -> none  [the longest x3 1.43 us: shards(): factor = jnp.linalg.cholesky(gram_matrix)]
    dot_general x5 -> x0, matrix products: 2.7 us -> none  [the longest x1 1.09 us: shards(): jnp.dot(vectors, lax.all_gather(prepared, 'dp', axis=0, tiled=True).T, pr...]
  transfers between devices with their start and end apart: 3 -> 0, of which waited for: 3 -> 0; matrix products, arithmetic and copies ran while one was open for 3% -> 0% of each run, Pallas kernels for 0% -> 0%
where the time goes in v1:
time: 25.9 us; the launch traced here: 25.7 us
  Pallas kernels  18.7 us (72%)
  local copies, waits for them, and re-layouts  6.95 us (27%)
    pallas_call x1, Pallas kernels, shards(): pl.pallas_call(functools.partial(kernel, sizes, chunks), out_shape=jax.Sh...  18.7 us
    unnamed x13, local copies, waits for them, and re-layouts  6.95 us

profile of v1, /device:TPU:0, one launch (start us, length us, event | category | flops | bytes accessed | tf_op | source)
XLA Modules:
  0.0 25.7 jit_solution(4815117898945346916)
XLA Ops:
  0.0 0.0 copy-start
  0.0 1.8 %copy-done = bf16[2,96,7168]{2,1,0:T(8,128)(2,1)S(1)} copy-done((bf16[2,96,7168]{2,1,0:T(8,128)(2,1)S(1)}, bf16[2,96,7168]{2,1,0:T(8,128)(2,1)}, u32[]{:S(2)}) %copy-start) | copy-done | bytes 2752536
  1.8 0.0 copy-start.1
  1.8 1.1 %copy-done.1 = bf16[2,96,2048]{2,1,0:T(8,128)(2,1)S(1)} copy-done((bf16[2,96,2048]{2,1,0:T(8,128)(2,1)S(1)}, bf16[2,96,2048]{2,1,0:T(8,128)(2,1)}, u32[]{:S(2)}) %copy-start.1) | copy-done | bytes 786456
  2.9 0.0 copy-start.2
  2.9 1.0 %copy-done.2 = bf16[32,7168]{1,0:T(8,128)(2,1)S(1)} copy-done((bf16[32,7168]{1,0:T(8,128)(2,1)S(1)}, bf16[32,7168]{1,0:T(8,128)(2,1)}, u32[]{:S(2)}) %copy-start.2) | copy-done | bytes 458776
  3.9 0.0 copy-start.3
  3.9 0.9 %copy-done.3 = bf16[32,2048]{1,0:T(8,128)(2,1)S(1)} copy-done((bf16[32,2048]{1,0:T(8,128)(2,1)S(1)}, bf16[32,2048]{1,0:T(8,128)(2,1)}, u32[]{:S(2)}) %copy-start.3) | copy-done | bytes 131096
  4.8 0.0 copy-start.4
  4.8 0.9 %copy-done.4 = f32[32,1024]{1,0:T(8,128)S(1)} copy-done((f32[32,1024]{1,0:T(8,128)S(1)}, f32[32,1024]{1,0:T(8,128)}, u32[]{:S(2)}) %copy-start.4) | copy-done | bytes 131096
  5.7 0.0 copy-start.5
  5.7 0.7 %copy-done.5 = s32[2]{0:T(128)S(1)} copy-done((s32[2]{0:T(128)S(1)}, s32[2]{0:T(128)}, u32[]{:S(2)}) %copy-start.5) | copy-done | bytes 32
  6.4 18.7 %shard_map.64 = f32[2,128]{1,0:T(2,128)S(1)} custom-call(bf16[2,96,7168]{2,1,0:T(8,128)(2,1)S(1)} %copy-done, bf16[2,96,2048]{2,1,0:T(8,128)(2,1)S(1)} %copy-done.1, bf16[32,7168]{1,0:T(8,128)(2,1)S(1)} %copy-done.2, bf16[32,2048]{1,0:T(8,128)(2,1)S(1)} %copy-done.3, s32[2]{0:T(128)S(1)} %copy-done.5, f32[32,1024]{1,0:T(8,128)S(1)} %copy-done.4), custom_call_target="tpu_custom_call" | custom-call | tf_op jit(solution)/shard_map/pallas_call | solution.py:296
  25.1 0.6 %copy.8 = f32[2,128]{1,0:T(2,128)} copy(f32[2,128]{1,0:T(2,128)S(1)} %shard_map.64) | data formatting | bytes 2048
Async XLA Ops:
  0.0 1.8 %copy-start = (bf16[2,96,7168]{2,1,0:T(8,128)(2,1)S(1)}, bf16[2,96,7168]{2,1,0:T(8,128)(2,1)}, u32[]{:S(2)}) copy-start(bf16[2,96,7168]{2,1,0:T(8,128)(2,1)} %hidden_hbm.1) | copy-start | bytes 8257540
  1.8 1.1 %copy-start.1 = (bf16[2,96,2048]{2,1,0:T(8,128)(2,1)S(1)}, bf16[2,96,2048]{2,1,0:T(8,128)(2,1)}, u32[]{:S(2)}) copy-start(bf16[2,96,2048]{2,1,0:T(8,128)(2,1)} %grad_hbm.1) | copy-start | bytes 2359300
  2.9 1.0 %copy-start.2 = (bf16[32,7168]{1,0:T(8,128)(2,1)S(1)}, bf16[32,7168]{1,0:T(8,128)(2,1)}, u32[]{:S(2)}) copy-start(bf16[32,7168]{1,0:T(8,128)(2,1)} %proj_in_hbm.1) | copy-start | bytes 1376260
  3.9 0.9 %copy-start.3 = (bf16[32,2048]{1,0:T(8,128)(2,1)S(1)}, bf16[32,2048]{1,0:T(8,128)(2,1)}, u32[]{:S(2)}) copy-start(bf16[32,2048]{1,0:T(8,128)(2,1)} %proj_out_hbm.1) | copy-start | bytes 393220
  4.8 0.9 %copy-start.4 = (f32[32,1024]{1,0:T(8,128)S(1)}, f32[32,1024]{1,0:T(8,128)}, u32[]{:S(2)}) copy-start(f32[32,1024]{1,0:T(8,128)} %query_hbm.1) | copy-start | bytes 393220
  5.7 0.7 %copy-start.5 = (s32[2]{0:T(128)S(1)}, s32[2]{0:T(128)}, u32[]{:S(2)}) copy-start(s32[2]{0:T(128)} %lengths_ref.1) | copy-start | bytes 28

commit v2 on v1

--- a/solution.py
+++ b/solution.py
@@ -80,13 +80,14 @@
     grad_hbm,
     proj_in_hbm,
     proj_out_hbm,
-    lengths_ref,
+    lengths_hbm,
     query_hbm,
     out_ref,
     hidden,
     grad,
     proj_in,
     proj_out,
+    lengths_ref,
     query,
     sums,
     pair,
@@ -133,6 +134,7 @@
             )
         )
     query_copy = load(query_hbm, query, load_sem.at[2])
+    lengths_copy = load(lengths_hbm, lengths_ref, load_sem.at[3])
 
     barrier = pltpu.get_barrier_semaphore()
 
@@ -182,8 +184,9 @@
             in_sums[e] += dot_last(proj_in[:, part], hidden[e, :, part])
     for e in range(examples):
         sums[1, e] = in_sums[e]
+    query_copy.wait()
+    lengths_copy.wait()
     in_exchange = exchange(1)
-    query_copy.wait()
     out_exchange.wait()
     positions = my_query * seq + lax.broadcasted_iota(jnp.int32, (1, seq), 1)
     weighted = []
@@ -296,20 +299,21 @@
     return pl.pallas_call(
         functools.partial(kernel, sizes, chunks),
         out_shape=jax.ShapeDtypeStruct((examples, dp_size * queries), jnp.float32),
-        in_specs=[hbm, hbm, hbm, hbm, pl.BlockSpec(memory_space=pltpu.SMEM), hbm],
+        in_specs=[hbm, hbm, hbm, hbm, hbm, hbm],
         out_specs=pl.BlockSpec(memory_space=pltpu.VMEM),
         scratch_shapes=[
             pltpu.VMEM(hidden_in.shape, hidden_in.dtype),
             pltpu.VMEM(out_grad.shape, out_grad.dtype),
             pltpu.VMEM(proj_in.shape, proj_in.dtype),
             pltpu.VMEM(proj_out.shape, proj_out.dtype),
+            pltpu.SMEM(lengths.shape, lengths.dtype),
             pltpu.VMEM(query_grads.shape, query_grads.dtype),
             sums,
             sums,
             pltpu.VMEM((planes, examples * pieces, LANES), jnp.float32),
             scores,
             scores,
-            dma((3,)),
+            dma((4,)),
             dma((2, chunks)),
             dma((2,)),
             dma((2,)),
@@ -321,7 +325,7 @@
         compiler_params=pltpu.CompilerParams(
             collective_id=0, has_side_effects=True, vmem_limit_bytes=32 * 1024 * 1024
         ),
-    )(hidden_in, out_grad, proj_in, proj_out, lengths, query_grads)
+    )(*(pltpu.with_memory_space_constraint(a, pltpu.HBM) for a in (hidden_in, out_grad, proj_in, proj_out, lengths, query_grads)))
 
 
 def solution(mesh):

time: 25.9 us -> 18.1 us (0.70)
  local copies, waits for them, and re-layouts: 6.95 us -> 0.56 us
  Pallas kernels: 18.7 us -> 17.4 us
    unnamed x13 -> x1, local copies, waits for them, and re-layouts: 6.95 us -> 0.56 us
    pallas_call x1, Pallas kernels: 18.7 us -> 17.4 us  [shards(): pl.pallas_call(functools.partial(kernel, sizes, chunks), out_shape=jax.Sh...]
where the time goes in v2:
time: 18.1 us; the launch traced here: 18 us
  Pallas kernels  17.4 us (96%)
  local copies, waits for them, and re-layouts  0.56 us (3%)
    pallas_call x1, Pallas kernels, shards(): pl.pallas_call(functools.partial(kernel, sizes, chunks), out_shape=jax.Sh...  17.4 us
    unnamed x1, local copies, waits for them, and re-layouts  0.56 us

profile of v2, /device:TPU:0, one launch (start us, length us, event | category | flops | bytes accessed | tf_op | source)
XLA Modules:
  0.0 18.0 jit_solution(12102363828816883832)
XLA Ops:
  0.0 17.4 %shard_map.64 = f32[2,128]{1,0:T(2,128)S(1)} custom-call(bf16[2,96,7168]{2,1,0:T(8,128)(2,1)} %hidden_hbm.1, bf16[2,96,2048]{2,1,0:T(8,128)(2,1)} %grad_hbm.1, bf16[32,7168]{1,0:T(8,128)(2,1)} %proj_in_hbm.1, bf16[32,2048]{1,0:T(8,128)(2,1)} %proj_out_hbm.1, s32[2]{0:T(128)} %lengths_hbm.1, f32[32,1024]{1,0:T(8,128)} %query_hbm.1), custom_call_target="tpu_custom_call" | custom-call | tf_op jit(solution)/shard_map/pallas_call | solution.py:299
  17.4 0.6 %copy.8 = f32[2,128]{1,0:T(2,128)} copy(f32[2,128]{1,0:T(2,128)S(1)} %shard_map.64) | data formatting | bytes 2048

commit v3 on v2

--- a/solution.py
+++ b/solution.py
@@ -30,11 +30,12 @@
 
 def solve_few(vectors, rhs, shift):
     total, width = rhs.shape
-    rows = lax.broadcasted_iota(jnp.int32, (total, width), 0)
+    rows = lax.broadcasted_iota(jnp.int32, (total, LANES), 0)
     columns = []
+    parts = [rhs[:, at : at + LANES] for at in range(0, width, LANES)]
     for j in range(total):
         column = jnp.sum(vectors * vectors[j : j + 1], axis=1, keepdims=True)
-        column = jnp.broadcast_to(column, (total, width))
+        column = jnp.broadcast_to(column, (total, LANES))
         columns.append(jnp.where(rows == j, column + shift, column))
     for k in range(total):
         pivot = columns[k]
@@ -44,9 +45,9 @@
             own = array[k : k + 1] * inverse
             return jnp.where(rows == k, own, array - pivot * own)
 
-        rhs = step(rhs)
+        parts = [step(part) for part in parts]
         columns = [step(c) if j > k else c for j, c in enumerate(columns)]
-    return rhs
+    return jnp.concatenate(parts, axis=1)
 
 
 def solve_many(vectors, rhs, shift):
@@ -102,6 +103,10 @@
     grads_recv,
     score_send,
     score_recv,
+    query_send,
+    query_recv,
+    share_send,
+    share_recv,
 ):
     dp_size, query_size, mp_size = sizes
     assert mp_size == 2
@@ -109,7 +114,9 @@
     other = 1 - my_mp
     examples, seq, width = hidden.shape
     rank = proj_in.shape[0]
-    queries = query.shape[0]
+    gathered = query.shape[0] == dp_size
+    queries = query.shape[1] * query.shape[2]
+    features = query.shape[3]
     planes = dp_size * query_size
     me = my_query * dp_size + my_dp
     total = dp_size * examples
@@ -133,7 +140,8 @@
                 load(hidden_hbm.at[:, :, part], hidden.at[:, :, part], hidden_sem.at[1, c]),
             )
         )
-    query_copy = load(query_hbm, query, load_sem.at[2])
+    own_query = my_dp if gathered else 0
+    query_copy = load(query_hbm, query.at[own_query], load_sem.at[2])
     lengths_copy = load(lengths_hbm, lengths_ref, load_sem.at[3])
 
     barrier = pltpu.get_barrier_semaphore()
@@ -158,7 +166,7 @@
     ).astype(jnp.bfloat16)
     grad_copy.wait()
     for e in range(examples):
-        sums[0, e] = dot_last(ordered, grad[e])
+        sums[0, e] = dot_last(grad[e], ordered).T
 
     pl.semaphore_wait(barrier, planes)
 
@@ -174,16 +182,41 @@
         copy.start()
         return copy
 
+    def query_to(slot, target):
+        return pltpu.make_async_remote_copy(
+            src_ref=query_hbm.at[my_mp],
+            dst_ref=query.at[slot, my_mp],
+            send_sem=query_send.at[target],
+            recv_sem=query_recv.at[slot],
+            device_id={"dp": target},
+            device_id_type=MESH,
+        )
+
+    def query_share(slot, half):
+        return pltpu.make_async_remote_copy(
+            src_ref=query.at[slot, half],
+            dst_ref=query.at[slot, half],
+            send_sem=share_send.at[slot],
+            recv_sem=share_recv.at[slot],
+            device_id={"mp": other},
+            device_id_type=MESH,
+        )
+
+    def dp_slot(step):
+        return lax.rem(my_dp + step, dp_size)
+
     out_exchange = exchange(0)
-    in_sums = [jnp.zeros((rank, seq), jnp.float32) for _ in range(examples)]
+    if gathered:
+        each(dp_size, lambda step: query_to(my_dp, dp_slot(step)).start())
+    in_sums = [jnp.zeros((seq, rank), jnp.float32) for _ in range(examples)]
     for c in range(chunks):
         for copy in hidden_copies[c]:
             copy.wait()
         part = pl.ds(c * step_width, step_width)
         for e in range(examples):
-            in_sums[e] += dot_last(proj_in[:, part], hidden[e, :, part])
+            in_sums[e] += dot_last(hidden[e, :, part], proj_in[:, part])
     for e in range(examples):
-        sums[1, e] = in_sums[e]
+        sums[1, e] = in_sums[e].T
     query_copy.wait()
     lengths_copy.wait()
     in_exchange = exchange(1)
@@ -230,6 +263,11 @@
         grads_copy(me, place(step)[0]).wait_send()
 
     each(planes, send_grads)
+    if gathered:
+        for step in range(1, dp_size):
+            slot = dp_slot(step)
+            query_to(slot, slot).wait_recv()
+            query_share(slot, my_mp).start()
     each(planes, wait_grads)
 
     pieces_of = []
@@ -241,11 +279,27 @@
         pieces_of.append(piece)
     vectors = jnp.concatenate(pieces_of, axis=1)
     blocks = LANES // queries
-    rhs = dot_last(
-        vectors, jnp.concatenate([query[...]] * blocks, axis=0), lax.Precision.HIGHEST
-    )
     shift = DAMPING * total
     solve = solve_few if total <= SUBLANES else solve_many
+    if gathered:
+        solved = solve(vectors, vectors * shift, shift)
+        for step in range(1, dp_size):
+            query_share(dp_slot(step), other).wait_recv()
+        scores = dot_last(
+            solved, query[...].reshape(dp_size * queries, features), lax.Precision.HIGHEST
+        )
+        mine = scores[:examples]
+        for d in range(1, dp_size):
+            mine = jnp.where(my_dp == d, scores[d * examples : (d + 1) * examples], mine)
+        out_ref[...] = mine
+        each(planes, wait_sent)
+        for step in range(1, dp_size):
+            query_to(my_dp, dp_slot(step)).wait_send()
+            query_share(dp_slot(step), my_mp).wait_send()
+        return
+    rhs = dot_last(
+        vectors, jnp.concatenate([query[0].reshape(queries, features)] * blocks, axis=0), lax.Precision.HIGHEST
+    )
     solved = solve(vectors, rhs * shift, shift)
     block_of_lane = lax.broadcasted_iota(jnp.int32, (total, LANES), 1) // queries
     solved = jnp.where(block_of_lane == lax.rem(my_dp, blocks), solved, 0.0)
@@ -285,10 +339,12 @@
 
 
 def shards(sizes, hidden_in, out_grad, proj_in, proj_out, lengths, query_grads):
-    dp_size, query_size, _ = sizes
+    dp_size, query_size, mp_size = sizes
     examples, seq, _ = hidden_in.shape
     rank = proj_in.shape[0]
     queries, flat = query_grads.shape
+    query_grads = query_grads.reshape(mp_size, queries // mp_size, flat)
+    held = dp_size if dp_size <= 4 else 1
     planes = dp_size * query_size
     pieces = flat // LANES
     chunks = 4
@@ -307,7 +363,7 @@
             pltpu.VMEM(proj_in.shape, proj_in.dtype),
             pltpu.VMEM(proj_out.shape, proj_out.dtype),
             pltpu.SMEM(lengths.shape, lengths.dtype),
-            pltpu.VMEM(query_grads.shape, query_grads.dtype),
+            pltpu.VMEM((held, *query_grads.shape), query_grads.dtype),
             sums,
             sums,
             pltpu.VMEM((planes, examples * pieces, LANES), jnp.float32),
@@ -321,6 +377,10 @@
             dma((planes,)),
             dma((dp_size,)),
             dma((dp_size,)),
+            dma((held,)),
+            dma((held,)),
+            dma((held,)),
+            dma((held,)),
         ],
         compiler_params=pltpu.CompilerParams(
             collective_id=0, has_side_effects=True, vmem_limit_bytes=32 * 1024 * 1024

time: 18.1 us -> 16.9 us (0.934)
  Pallas kernels: 17.4 us -> 16.2 us
    pallas_call x1, Pallas kernels: 17.4 us -> 16.2 us  [shards(): pl.pallas_call(functools.partial(kernel, sizes, chunks), out_shape=jax.Sh...]
where the time goes in v3:
time: 16.9 us; the launch traced here: 16.8 us
  Pallas kernels  16.2 us (96%)
  local copies, waits for them, and re-layouts  0.56 us (3%)
    pallas_call x1, Pallas kernels, shards(): pl.pallas_call(functools.partial(kernel, sizes, chunks), out_shape=jax.Sh...  16.2 us
    unnamed x1, local copies, waits for them, and re-layouts  0.56 us

profile of v3, /device:TPU:0, one launch (start us, length us, event | category | flops | bytes accessed | tf_op | source)
XLA Modules:
  0.0 16.8 jit_solution(1722847029834663711)
XLA Ops:
  0.0 16.2 %shard_map.64 = f32[2,128]{1,0:T(2,128)S(1)} custom-call(bf16[2,96,7168]{2,1,0:T(8,128)(2,1)} %hidden_hbm.1, bf16[2,96,2048]{2,1,0:T(8,128)(2,1)} %grad_hbm.1, bf16[32,7168]{1,0:T(8,128)(2,1)} %proj_in_hbm.1, bf16[32,2048]{1,0:T(8,128)(2,1)} %proj_out_hbm.1, s32[2]{0:T(128)} %lengths_hbm.1, f32[2,16,1024]{2,1,0:T(8,128)} %bitcast.1), custom_call_target="tpu_custom_call" | custom-call | tf_op jit(solution)/shard_map/pallas_call | solution.py:355
  16.2 0.6 %copy.8 = f32[2,128]{1,0:T(2,128)} copy(f32[2,128]{1,0:T(2,128)S(1)} %shard_map.64) | data formatting | bytes 2048

commit v4 on v3

--- a/solution.py
+++ b/solution.py
@@ -18,6 +18,16 @@
     return lax.dot_general(
         left, right, LAST, precision=precision, preferred_element_type=jnp.float32
     )
+
+
+def dot_split(left, right):
+    lefts, rights = [], []
+    for array, parts in ((left, lefts), (right, rights)):
+        high = array.astype(jnp.bfloat16)
+        parts += [high, (array - high.astype(jnp.float32)).astype(jnp.bfloat16)]
+    rows = left.shape[0]
+    both = dot_last(jnp.concatenate(lefts, axis=0), rights[0])
+    return both[:rows] + (both[rows:] + dot_last(lefts[0], rights[1]))
 
 
 def each(count, body):
@@ -156,6 +166,46 @@
     pl.semaphore_signal(barrier, inc=1, device_id={"mp": other}, device_id_type=MESH)
     each(planes, greet)
 
+    pl.semaphore_wait(barrier, planes)
+
+    def exchange(which):
+        copy = pltpu.make_async_remote_copy(
+            src_ref=sums.at[which],
+            dst_ref=pair.at[which],
+            send_sem=pair_send.at[which],
+            recv_sem=pair_recv.at[which],
+            device_id={"mp": other},
+            device_id_type=MESH,
+        )
+        copy.start()
+        return copy
+
+    def query_to(slot, target):
+        return pltpu.make_async_remote_copy(
+            src_ref=query_hbm.at[my_mp],
+            dst_ref=query.at[slot, my_mp],
+            send_sem=query_send.at[target],
+            recv_sem=query_recv.at[slot],
+            device_id={"dp": target},
+            device_id_type=MESH,
+        )
+
+    def query_share(slot, half):
+        return pltpu.make_async_remote_copy(
+            src_ref=query.at[slot, half],
+            dst_ref=query.at[slot, half],
+            send_sem=share_send.at[slot],
+            recv_sem=share_recv.at[slot],
+            device_id={"mp": other},
+            device_id_type=MESH,
+        )
+
+    def dp_slot(step):
+        return lax.rem(my_dp + step, dp_size)
+
+    if gathered:
+        each(dp_size, lambda step: query_to(my_dp, dp_slot(step)).start())
+
     proj_out_copy.wait()
     to_row = lax.broadcasted_iota(jnp.int32, (rank, rank), 0)
     from_row = lax.broadcasted_iota(jnp.int32, (rank, rank), 1)
@@ -168,46 +218,7 @@
     for e in range(examples):
         sums[0, e] = dot_last(grad[e], ordered).T
 
-    pl.semaphore_wait(barrier, planes)
-
-    def exchange(which):
-        copy = pltpu.make_async_remote_copy(
-            src_ref=sums.at[which],
-            dst_ref=pair.at[which],
-            send_sem=pair_send.at[which],
-            recv_sem=pair_recv.at[which],
-            device_id={"mp": other},
-            device_id_type=MESH,
-        )
-        copy.start()
-        return copy
-
-    def query_to(slot, target):
-        return pltpu.make_async_remote_copy(
-            src_ref=query_hbm.at[my_mp],
-            dst_ref=query.at[slot, my_mp],
-            send_sem=query_send.at[target],
-            recv_sem=query_recv.at[slot],
-            device_id={"dp": target},
-            device_id_type=MESH,
-        )
-
-    def query_share(slot, half):
-        return pltpu.make_async_remote_copy(
-            src_ref=query.at[slot, half],
-            dst_ref=query.at[slot, half],
-            send_sem=share_send.at[slot],
-            recv_sem=share_recv.at[slot],
-            device_id={"mp": other},
-            device_id_type=MESH,
-        )
-
-    def dp_slot(step):
-        return lax.rem(my_dp + step, dp_size)
-
     out_exchange = exchange(0)
-    if gathered:
-        each(dp_size, lambda step: query_to(my_dp, dp_slot(step)).start())
     in_sums = [jnp.zeros((seq, rank), jnp.float32) for _ in range(examples)]
     for c in range(chunks):
         for copy in hidden_copies[c]:
@@ -285,9 +296,7 @@
         solved = solve(vectors, vectors * shift, shift)
         for step in range(1, dp_size):
             query_share(dp_slot(step), other).wait_recv()
-        scores = dot_last(
-            solved, query[...].reshape(dp_size * queries, features), lax.Precision.HIGHEST
-        )
+        scores = dot_split(solved, query[...].reshape(dp_size * queries, features))
         mine = scores[:examples]
         for d in range(1, dp_size):
             mine = jnp.where(my_dp == d, scores[d * examples : (d + 1) * examples], mine)

time: 16.9 us -> 16 us (0.947)
  Pallas kernels: 16.2 us -> 15.2 us
    pallas_call x1, Pallas kernels: 16.2 us -> 15.2 us  [shards(): pl.pallas_call(functools.partial(kernel, sizes, chunks), out_shape=jax.Sh...]
where the time goes in v4:
time: 16 us; the launch traced here: 15.8 us
  Pallas kernels  15.2 us (95%)
  local copies, waits for them, and re-layouts  0.56 us (4%)
    pallas_call x1, Pallas kernels, shards(): pl.pallas_call(functools.partial(kernel, sizes, chunks), out_shape=jax.Sh...  15.2 us
    unnamed x1, local copies, waits for them, and re-layouts  0.56 us

profile of v4, /device:TPU:0, one launch (start us, length us, event | category | flops | bytes accessed | tf_op | source)
XLA Modules:
  0.0 15.8 jit_solution(17784505081272631734)
XLA Ops:
  0.0 15.2 %shard_map.64 = f32[2,128]{1,0:T(2,128)S(1)} custom-call(bf16[2,96,7168]{2,1,0:T(8,128)(2,1)} %hidden_hbm.1, bf16[2,96,2048]{2,1,0:T(8,128)(2,1)} %grad_hbm.1, bf16[32,7168]{1,0:T(8,128)(2,1)} %proj_in_hbm.1, bf16[32,2048]{1,0:T(8,128)(2,1)} %proj_out_hbm.1, s32[2]{0:T(128)} %lengths_hbm.1, f32[2,16,1024]{2,1,0:T(8,128)} %bitcast.1), custom_call_target="tpu_custom_call" | custom-call | tf_op jit(solution)/shard_map/pallas_call | solution.py:364
  15.2 0.6 %copy.8 = f32[2,128]{1,0:T(2,128)} copy(f32[2,128]{1,0:T(2,128)S(1)} %shard_map.64) | data formatting | bytes 2048

commit v5 on v4

--- a/solution.py
+++ b/solution.py
@@ -124,9 +124,9 @@
     other = 1 - my_mp
     examples, seq, width = hidden.shape
     rank = proj_in.shape[0]
-    gathered = query.shape[0] == dp_size
-    queries = query.shape[1] * query.shape[2]
-    features = query.shape[3]
+    gathered = query.shape[0] == dp_size == 4
+    queries = query.shape[1] * query.shape[2] * query.shape[3]
+    features = query.shape[4]
     planes = dp_size * query_size
     me = my_query * dp_size + my_dp
     total = dp_size * examples
@@ -180,12 +180,16 @@
         copy.start()
         return copy
 
-    def query_to(slot, target):
+    beside = my_dp + 1 - 2 * lax.rem(my_dp, 2)
+    across = lax.rem(my_dp + 2, 4)
+    middle = (my_dp == 1) | (my_dp == 2)
+
+    def query_to(which, half, slot, target, source=None):
         return pltpu.make_async_remote_copy(
-            src_ref=query_hbm.at[my_mp],
-            dst_ref=query.at[slot, my_mp],
-            send_sem=query_send.at[target],
-            recv_sem=query_recv.at[slot],
+            src_ref=query_hbm.at[my_mp, half] if source is None else source,
+            dst_ref=query.at[slot, my_mp, half],
+            send_sem=query_send.at[which, half],
+            recv_sem=query_recv.at[which, half],
             device_id={"dp": target},
             device_id_type=MESH,
         )
@@ -204,7 +208,16 @@
         return lax.rem(my_dp + step, dp_size)
 
     if gathered:
-        each(dp_size, lambda step: query_to(my_dp, dp_slot(step)).start())
+        query_to(0, 0, my_dp, 3 - my_dp).start()
+        query_to(0, 1, my_dp, 3 - my_dp).start()
+
+        @pl.when(jnp.logical_not(middle))
+        def _():
+            query_to(2, 0, my_dp, across).start()
+
+        query_to(2, 1, my_dp, across).start()
+        for half in range(2):
+            query_to(1, half, my_dp, beside).start()
 
     proj_out_copy.wait()
     to_row = lax.broadcasted_iota(jnp.int32, (rank, rank), 0)
@@ -275,10 +288,21 @@
 
     each(planes, send_grads)
     if gathered:
-        for step in range(1, dp_size):
-            slot = dp_slot(step)
-            query_to(slot, slot).wait_recv()
-            query_share(slot, my_mp).start()
+        query_to(0, 0, 3 - my_dp, 3 - my_dp).wait_recv()
+
+        @pl.when(middle)
+        def _():
+            inner = 3 - my_dp
+            query_to(2, 0, inner, beside, query.at[inner, my_mp, 0]).start()
+
+        query_to(0, 1, 3 - my_dp, 3 - my_dp).wait_recv()
+        query_share(3 - my_dp, my_mp).start()
+        for half in range(2):
+            query_to(1, half, beside, beside).wait_recv()
+        query_share(beside, my_mp).start()
+        for half in range(2):
+            query_to(2, half, across, across).wait_recv()
+        query_share(across, my_mp).start()
     each(planes, wait_grads)
 
     pieces_of = []
@@ -303,7 +327,8 @@
         out_ref[...] = mine
         each(planes, wait_sent)
         for step in range(1, dp_size):
-            query_to(my_dp, dp_slot(step)).wait_send()
+            for half in range(2):
+                query_to(step - 1, half, my_dp, dp_slot(step)).wait_send()
             query_share(dp_slot(step), my_mp).wait_send()
         return
     rhs = dot_last(
@@ -352,8 +377,8 @@
     examples, seq, _ = hidden_in.shape
     rank = proj_in.shape[0]
     queries, flat = query_grads.shape
-    query_grads = query_grads.reshape(mp_size, queries // mp_size, flat)
-    held = dp_size if dp_size <= 4 else 1
+    query_grads = query_grads.reshape(mp_size, 2, queries // mp_size // 2, flat)
+    held = dp_size if dp_size == 4 else 1
     planes = dp_size * query_size
     pieces = flat // LANES
     chunks = 4
@@ -386,8 +411,8 @@
             dma((planes,)),
             dma((dp_size,)),
             dma((dp_size,)),
-            dma((held,)),
-            dma((held,)),
+            dma((3, 2)),
+            dma((3, 2)),
             dma((held,)),
             dma((held,)),
         ],

time: 16 us -> 16 us (level)
  the two profiles are of different devices: /device:TPU:0 before, /device:TPU:1 now
where the time goes in v5:
time: 16 us; the launch traced here: 15.9 us
  Pallas kernels  15.3 us (96%)
  local copies, waits for them, and re-layouts  0.56 us (4%)
    pallas_call x1, Pallas kernels, shards(): pl.pallas_call(functools.partial(kernel, sizes, chunks), out_shape=jax.Sh...  15.3 us
    unnamed x1, local copies, waits for them, and re-layouts  0.56 us

profile of v5, /device:TPU:1, one launch (start us, length us, event | category | flops | bytes accessed | tf_op | source)
XLA Modules:
  0.0 15.9 jit_solution(10330290915003253651)
XLA Ops:
  0.0 15.3 %shard_map.64 = f32[2,128]{1,0:T(2,128)S(1)} custom-call(bf16[2,96,7168]{2,1,0:T(8,128)(2,1)} %hidden_hbm.1, bf16[2,96,2048]{2,1,0:T(8,128)(2,1)} %grad_hbm.1, bf16[32,7168]{1,0:T(8,128)(2,1)} %proj_in_hbm.1, bf16[32,2048]{1,0:T(8,128)(2,1)} %proj_out_hbm.1, s32[2]{0:T(128)} %lengths_hbm.1, f32[2,2,8,1024]{3,2,1,0:T(8,128)} %bitcast.1), custom_call_target="tpu_custom_call" | custom-call | tf_op jit(solution)/shard_map/pallas_call | solution.py:389
  15.3 0.6 %copy.8 = f32[2,128]{1,0:T(2,128)} copy(f32[2,128]{1,0:T(2,128)S(1)} %shard_map.64) | data formatting | bytes 2048
